TPU v7x, 32 devices: a whole 2x2x4 slice. The times are simulated.
32 devices in a mesh: dp: 8 (over z, y), feat: 4 (over x, core).
Axes of the slice: x: 2, y: 2, z: 4, core: 2. Of those that a mesh axis runs over, the one named last changes fastest.
Arguments:
- first_view_outputs: bfloat16 [512, 8192], P('dp', 'feat'), may hold values from -120 to 120
- second_view_outputs: bfloat16 [512, 8192], P('feat', 'dp'), may hold values from -120 to 120
Outputs:
- first_view_gradient: bfloat16 [512, 8192], P('dp', 'feat')
- second_view_gradient: bfloat16 [512, 8192], P('feat', 'dp')
All inputs are finite; a program needn't handle non-finite values.
Results may differ from a plain program's by a relative error of at most 0.033.
Values may be sent and summed in bfloat16 or wider, within the bound.
A program may use at most 64 MiB of HBM per device.

v0:
```python
import functools
import jax
import jax.numpy as jnp
from jax import lax
from jax.experimental import pallas as pl
from jax.experimental.pallas import tpu as pltpu
from jax.sharding import PartitionSpec as P

EPSILON = 1e-05
OFF_WEIGHT = 0.0051
MESH = pl.DeviceIdType.MESH
BLK = 128
GROUP = 4


def normalize_backward(
    normalized_gradient, standardized_values, inverse_scale, column_sums, total_count
):
    centering_term = column_sums[0] / total_count
    projection_term = column_sums[1] / total_count
    return (
        (normalized_gradient - centering_term - standardized_values * projection_term)
        * inverse_scale
    ).astype(jnp.bfloat16)


def general_shards(first_view_outputs, second_view_outputs):
    rows_a, width_a = first_view_outputs.shape
    rows_b, width_b = second_view_outputs.shape
    total_count = rows_a * lax.axis_size("dp")

    def standardize(values, axis):
        local = values.astype(jnp.float32)
        center = lax.psum(jnp.sum(local, axis=0), axis) / total_count
        centered = local - center
        spread = lax.psum(jnp.sum(centered * centered, axis=0), axis) / total_count
        inverse = lax.rsqrt(spread + EPSILON)
        standardized = centered * inverse
        gathered = lax.all_gather(standardized.astype(jnp.bfloat16), axis, axis=0, tiled=True)
        return standardized, inverse, gathered

    standardized_first, inverse_first, normalized_first = standardize(first_view_outputs, "dp")
    standardized_second, inverse_second, normalized_second = standardize(
        second_view_outputs, "feat"
    )
    correlation = (
        lax.dot_general(
            normalized_first,
            normalized_second,
            (((0,), (0,)), ((), ())),
            preferred_element_type=jnp.float32,
        )
        / total_count
    )
    row_ids = lax.axis_index("feat") * width_a + lax.broadcasted_iota(
        jnp.int32, (width_a, width_b), 0
    )
    col_ids = lax.axis_index("dp") * width_b + lax.broadcasted_iota(
        jnp.int32, (width_a, width_b), 1
    )
    grad_tile = jnp.where(
        row_ids == col_ids, 2.0 * (correlation - 1.0), 2.0 * OFF_WEIGHT * correlation
    ).astype(jnp.bfloat16)

    def finish(partial, axis, standardized, inverse):
        gradient = lax.psum_scatter(
            partial.astype(jnp.bfloat16), axis, scatter_dimension=0, tiled=True
        ).astype(jnp.float32)
        sums = lax.psum(
            (jnp.sum(gradient, axis=0), jnp.sum(gradient * standardized, axis=0)), axis
        )
        return normalize_backward(gradient, standardized, inverse, sums, total_count)

    partial_first = lax.dot_general(
        normalized_second,
        grad_tile,
        (((1,), (1,)), ((), ())),
        preferred_element_type=jnp.float32,
    )
    partial_second = jnp.dot(normalized_first, grad_tile, preferred_element_type=jnp.float32)
    return (
        finish(partial_first, "dp", standardized_first, inverse_first),
        finish(partial_second, "feat", standardized_second, inverse_second),
    )


def kernel(
    features,
    chunk,
    a_ref,
    b_ref,
    ga_ref,
    gb_ref,
    raw,
    xhat,
    inv,
    norm,
    other,
    base,
    running,
    packed,
    r1,
    s1,
    r2,
    gathered,
    full_packed,
    gram,
    grad,
    relay,
    in_send,
    in_recv,
    swap_send,
    swap_recv,
    rs1_send,
    rs1_recv,
    rs2_send,
    rs2_recv,
    ag1_send,
    ag1_recv,
    ag2_send,
    ag2_recv,
    out_send,
    out_recv,
    relay_send,
    relay_recv,
):
    n_dp, n_feat = 8, 4
    n_dev = n_dp * n_feat
    p = lax.axis_index("dp")
    f = lax.axis_index("feat")
    z, y = p // 2, p % 2
    x, core = f // 2, f % 2
    g = 2 * y + x
    rows_a = a_ref.shape[0]
    rows_b = b_ref.shape[0]
    count, width = raw.shape
    n_chunks = width // chunk
    n_blk = count // BLK
    seg = packed.shape[0] // GROUP
    unit = seg // GROUP

    barrier = pltpu.get_barrier_semaphore()
    for dp_to in reversed(range(n_dp)):
        for feat_to in range(n_feat):

            @pl.when(jnp.logical_or(p != dp_to, f != feat_to))
            def _():
                pl.semaphore_signal(
                    barrier, inc=1, device_id=(dp_to, feat_to), device_id_type=MESH
                )

    pl.semaphore_wait(barrier, n_dev - 1)

    def start_or_local(src, dst, send_sem, recv_sem, device, is_self):
        cp = pltpu.make_async_remote_copy(
            src_ref=src,
            dst_ref=dst,
            send_sem=send_sem,
            recv_sem=recv_sem,
            device_id=device,
            device_id_type=MESH,
        )

        @pl.when(is_self)
        def _():
            pltpu.make_async_copy(src, dst, recv_sem).start()

        @pl.when(jnp.logical_not(is_self))
        def _():
            cp.start()

        return cp, is_self

    def wait_sent(item):
        cp, is_self = item

        @pl.when(jnp.logical_not(is_self))
        def _():
            cp.wait_send()

    def piece_of_a(c, q):
        return a_ref.at[:, pl.ds(pl.multiple_of(q * width + c * chunk, chunk), chunk)]

    def rows_for_a(c):
        return raw.at[
            pl.ds(pl.multiple_of(p * rows_a, rows_a), rows_a), pl.ds(c * chunk, chunk)
        ]

    sent = []
    crossing = []
    for c in range(n_chunks):
        for ys in range(2):
            cp = pltpu.make_async_remote_copy(
                src_ref=piece_of_a(c, 2 * ys + 1 - x),
                dst_ref=relay.at[c, ys],
                send_sem=relay_send.at[c, ys],
                recv_sem=relay_recv.at[c, ys],
                device_id=(p, 2 * (1 - x) + core),
                device_id_type=MESH,
            )
            cp.start()
            crossing.append(cp)
        for k in range(2):
            y_to = (y + 1 + k) % 2
            dp_to = 2 * f + y_to
            sent.append(
                start_or_local(
                    piece_of_a(c, 2 * y_to + x),
                    rows_for_a(c),
                    in_send.at[c, k],
                    in_recv.at[c],
                    (dp_to, 2 * x),
                    jnp.logical_and(dp_to == p, core == 0),
                )
            )
    for c in range(n_chunks):
        for k in range(2):
            x_to = (x + 1 + k) % 2
            feat_to = 2 * x_to + 1
            sent.append(
                start_or_local(
                    b_ref.at[:, pl.ds(pl.multiple_of(x_to * width + c * chunk, chunk), chunk)],
                    raw.at[
                        pl.ds(pl.multiple_of(f * rows_b, rows_b), rows_b),
                        pl.ds(c * chunk, chunk),
                    ],
                    in_send.at[c, GROUP + k],
                    in_recv.at[c],
                    (p, feat_to),
                    feat_to == f,
                )
            )
    for c in range(n_chunks):
        for ys in range(2):
            crossing[2 * c + ys].wait_recv()
            dp_to = 2 * (2 * (1 - x) + core) + ys
            sent.append(
                start_or_local(
                    relay.at[c, ys],
                    rows_for_a(c),
                    in_send.at[c, 2 + ys],
                    in_recv.at[c],
                    (dp_to, 2 * x),
                    jnp.logical_and(dp_to == p, core == 0),
                )
            )

    eye = jnp.where(
        lax.broadcasted_iota(jnp.int32, (BLK, BLK), 0)
        == lax.broadcasted_iota(jnp.int32, (BLK, BLK), 1),
        jnp.float32(width),
        jnp.float32(0),
    )
    where = {}
    for bi in range(n_blk):
        for bj in range(bi, n_blk):
            where[bi, bj] = len(where)
    swaps = []
    for c in range(n_chunks):
        part = raw.at[:, pl.ds(c * chunk, chunk)]
        pltpu.make_async_copy(part, part, in_recv.at[c]).wait()
        for h in range(c * chunk, (c + 1) * chunk, BLK):
            cols = slice(h, h + BLK)
            values = raw[:, cols].astype(jnp.float32)
            center = jnp.sum(values, axis=0, keepdims=True) / count
            centered = values - center
            spread = jnp.sum(centered * centered, axis=0, keepdims=True) / count
            inverse = lax.rsqrt(spread + EPSILON)
            standardized = centered * inverse
            xhat[:, cols] = standardized
            norm[:, cols] = standardized.astype(jnp.bfloat16)
            inv[0:1, cols] = inverse
        cols = slice(c * chunk, (c + 1) * chunk)
        for bi in range(n_blk):
            share = lax.dot_general(
                norm[bi * BLK : (bi + 1) * BLK, cols],
                norm[bi * BLK :, cols],
                (((1,), (1,)), ((), ())),
                preferred_element_type=jnp.float32,
            )
            for bj in range(bi, n_blk):
                at = slice(where[bi, bj] * BLK, (where[bi, bj] + 1) * BLK)
                block = share[:, (bj - bi) * BLK : (bj - bi + 1) * BLK]
                if bi == bj and c == 0:
                    block = block - eye
                if c > 0:
                    block = block + running[at, :]
                if c < n_chunks - 1:
                    running[at, :] = block
                else:
                    packed[at, :] = block.astype(jnp.bfloat16)
        swap = pltpu.make_async_remote_copy(
            src_ref=norm.at[:, pl.ds(c * chunk, chunk)],
            dst_ref=other.at[:, pl.ds(c * chunk, chunk)],
            send_sem=swap_send.at[c],
            recv_sem=swap_recv.at[c],
            device_id=(p, 2 * x + 1 - core),
            device_id_type=MESH,
        )
        swaps.append(swap)
        if c < n_chunks - 1:
            swap.start()

    copies = []
    arriving = {}
    for kz in range(1, GROUP + 1):
        zt = (z + kz) % GROUP
        for k in range(1, GROUP):
            q = (g + k) % GROUP
            cp = pltpu.make_async_remote_copy(
                src_ref=packed.at[pl.ds(pl.multiple_of(q * seg + zt * unit, unit), unit), :],
                dst_ref=r1.at[kz - 1, k - 1],
                send_sem=rs1_send.at[kz - 1, k - 1],
                recv_sem=rs1_recv.at[kz - 1, k - 1],
                device_id=(2 * z + q // 2, 2 * (q % 2) + core),
                device_id_type=MESH,
            )
            cp.start()
            arriving[kz, k] = cp
            copies.append(cp)
    swaps[-1].start()
    coming = []
    for kz in range(1, GROUP + 1):
        zt = (z + kz) % GROUP
        total = packed[pl.ds(pl.multiple_of(g * seg + zt * unit, unit), unit), :].astype(
            jnp.float32
        )
        for k in range(1, GROUP):
            arriving[kz, k].wait_recv()
            total = total + r1[kz - 1, k - 1].astype(jnp.float32)
        if kz < GROUP:
            s1[kz - 1] = total.astype(jnp.bfloat16)
            cp = pltpu.make_async_remote_copy(
                src_ref=s1.at[kz - 1],
                dst_ref=r2.at[kz - 1],
                send_sem=rs2_send.at[kz - 1],
                recv_sem=rs2_recv.at[kz - 1],
                device_id=(2 * zt + y, f),
                device_id_type=MESH,
            )
            cp.start()
            coming.append(cp)
    for kz in range(1, GROUP):
        coming[kz - 1].wait_recv()
        total = total + r2[kz - 1].astype(jnp.float32)
    copies += coming
    mine = pl.ds(pl.multiple_of(z * unit, unit), unit)
    gathered[mine, :] = total.astype(jnp.bfloat16)

    coming = []
    for kz in range(1, GROUP):
        zt = (z + kz) % GROUP
        cp = pltpu.make_async_remote_copy(
            src_ref=gathered.at[mine, :],
            dst_ref=gathered.at[mine, :],
            send_sem=ag1_send.at[kz - 1],
            recv_sem=ag1_recv.at[kz - 1],
            device_id=(2 * zt + y, f),
            device_id_type=MESH,
        )
        cp.start()
        coming.append(cp)
    last = []
    for kz in range(GROUP):
        if kz > 0:
            coming[kz - 1].wait_recv()
        zs = (z + GROUP - kz) % GROUP
        for k in range(1, GROUP + 1):
            q = (g + k) % GROUP
            cp = pltpu.make_async_remote_copy(
                src_ref=gathered.at[pl.ds(pl.multiple_of(zs * unit, unit), unit), :],
                dst_ref=full_packed.at[
                    pl.ds(pl.multiple_of(g * seg + zs * unit, unit), unit), :
                ],
                send_sem=ag2_send.at[kz, k - 1],
                recv_sem=ag2_recv.at[kz, k - 1],
                device_id=(2 * z + q // 2, 2 * (q % 2) + 1 - core),
                device_id_type=MESH,
            )
            cp.start()
            last.append(cp)
    copies += coming

    scale = 2.0 * OFF_WEIGHT / count
    for c in range(n_chunks):
        swaps[c].wait_recv()
        cols = slice(c * chunk, (c + 1) * chunk)
        own = norm[:, cols].astype(jnp.float32)
        paired = other[:, cols].astype(jnp.float32)
        corr = jnp.sum(own * paired, axis=0, keepdims=True) / count
        diagonal = 2.0 * (corr - 1.0) - 2.0 * OFF_WEIGHT * corr
        base[:, cols] = own * (scale * features) + paired * diagonal
    for cp in last:
        cp.wait_recv()
    for (bi, bj), at in where.items():
        block = full_packed[at * BLK : (at + 1) * BLK, :]
        gram[bi * BLK : (bi + 1) * BLK, bj * BLK : (bj + 1) * BLK] = block
        if bi != bj:
            gram[bj * BLK : (bj + 1) * BLK, bi * BLK : (bi + 1) * BLK] = block.T

    for c in range(n_chunks):
        cols = slice(c * chunk, (c + 1) * chunk)
        dnorm = base[:, cols] + scale * lax.dot_general(
            gram[...], norm[:, cols], (((1,), (0,)), ((), ())), preferred_element_type=jnp.float32
        )
        standardized = xhat[:, cols]
        centering = jnp.sum(dnorm, axis=0, keepdims=True) / count
        projection = jnp.sum(dnorm * standardized, axis=0, keepdims=True) / count
        grad[:, cols] = (
            (dnorm - centering - standardized * projection) * inv[0:1, cols]
        ).astype(jnp.bfloat16)

        @pl.when(core == 0)
        def _():
            place = pl.ds(pl.multiple_of(g * width + c * chunk, chunk), chunk)
            for k in range(1, n_dp + 1):
                to = (p + k) % n_dp
                is_self = jnp.logical_and(to == p, z == f)
                src = grad.at[pl.ds(pl.multiple_of(to * rows_a, rows_a), rows_a), cols]

                start_or_local(
                    src,
                    ga_ref.at[:, place],
                    out_send.at[c, k - 1],
                    out_recv.at[0],
                    (to, z),
                    is_self,
                )

        @pl.when(core == 1)
        def _():
            place = pl.ds(pl.multiple_of(x * width + c * chunk, chunk), chunk)
            for k in range(1, n_feat + 1):
                to = (f + k) % n_feat
                src = grad.at[pl.ds(pl.multiple_of(to * rows_b, rows_b), rows_b), cols]
                if k == n_feat:
                    pltpu.make_async_copy(src, gb_ref.at[:, place], out_recv.at[1]).start()
                else:
                    pltpu.make_async_remote_copy(
                        src_ref=src,
                        dst_ref=gb_ref.at[:, place],
                        send_sem=out_send.at[c, k - 1],
                        recv_sem=out_recv.at[1],
                        device_id=(p, to),
                        device_id_type=MESH,
                    ).start()

    for item in sent:
        wait_sent(item)
    for cp in crossing + swaps + copies + last:
        cp.wait_send()

    @pl.when(core == 0)
    def _():
        for c in range(n_chunks):
            for k in range(1, n_dp + 1):
                to = (p + k) % n_dp
                piece = grad.at[0:rows_a, 0:chunk]

                @pl.when(jnp.logical_not(jnp.logical_and(to == p, z == f)))
                def _():
                    pltpu.make_async_copy(piece, piece, out_send.at[c, k - 1]).wait()

    @pl.when(core == 1)
    def _():
        for c in range(n_chunks):
            for k in range(1, n_feat):
                piece = grad.at[0:rows_b, 0:chunk]
                pltpu.make_async_copy(piece, piece, out_send.at[c, k - 1]).wait()

    pltpu.make_async_copy(ga_ref, ga_ref, out_recv.at[0]).wait()
    pltpu.make_async_copy(gb_ref, gb_ref, out_recv.at[1]).wait()


def hand_out(landed_a, landed_b, ga_ref, gb_ref, held_a, held_b, loads, stores):
    moves = ((landed_a, held_a, ga_ref), (landed_b, held_b, gb_ref))
    fetched = [
        pltpu.make_async_copy(src, held, loads.at[i]) for i, (src, held, _) in enumerate(moves)
    ]
    written = [
        pltpu.make_async_copy(held, dst, stores.at[i]) for i, (_, held, dst) in enumerate(moves)
    ]
    for cp in fetched:
        cp.start()
    for first, second in zip(fetched, written):
        first.wait()
        second.start()
    for cp in written:
        cp.wait()


def owned_shards(first_view_outputs, second_view_outputs):
    count = first_view_outputs.shape[0] * lax.axis_size("dp")
    features = first_view_outputs.shape[1] * lax.axis_size("feat")
    width = first_view_outputs.shape[1] // GROUP
    chunk = 256 if width % 256 == 0 else 128
    chunks = width // chunk
    n_blk = count // BLK
    packed_rows = n_blk * (n_blk + 1) // 2 * BLK
    seg = packed_rows // GROUP
    unit = seg // GROUP
    bf16, f32 = jnp.bfloat16, jnp.float32
    dma = pltpu.SemaphoreType.DMA
    any_spec = pl.BlockSpec(memory_space=pl.ANY)
    landed = pl.pallas_call(
        functools.partial(kernel, float(features), chunk),
        out_shape=[
            pltpu.VMEM(first_view_outputs.shape, bf16),
            pltpu.VMEM(second_view_outputs.shape, bf16),
        ],
        in_specs=[any_spec] * 2,
        out_specs=[pl.BlockSpec(memory_space=pltpu.VMEM)] * 2,
        scratch_shapes=[
            pltpu.VMEM((count, width), bf16),
            pltpu.VMEM((count, width), f32),
            pltpu.VMEM((8, width), f32),
            pltpu.VMEM((count, width), bf16),
            pltpu.VMEM((count, width), bf16),
            pltpu.VMEM((count, width), f32),
            pltpu.VMEM((packed_rows, BLK), f32),
            pltpu.VMEM((packed_rows, BLK), bf16),
            pltpu.VMEM((GROUP, GROUP - 1, unit, BLK), bf16),
            pltpu.VMEM((GROUP - 1, unit, BLK), bf16),
            pltpu.VMEM((GROUP - 1, unit, BLK), bf16),
            pltpu.VMEM((seg, BLK), bf16),
            pltpu.VMEM((packed_rows, BLK), bf16),
            pltpu.VMEM((count, count), bf16),
            pltpu.VMEM((count, width), bf16),
            pltpu.VMEM((chunks, 2, first_view_outputs.shape[0], chunk), bf16),
            dma((chunks, GROUP + 2)),
            dma((chunks,)),
            dma((chunks,)),
            dma((chunks,)),
            dma((GROUP, GROUP - 1)),
            dma((GROUP, GROUP - 1)),
            dma((GROUP - 1,)),
            dma((GROUP - 1,)),
            dma((GROUP - 1,)),
            dma((GROUP - 1,)),
            dma((GROUP, GROUP)),
            dma((GROUP, GROUP)),
            dma((chunks, 8)),
            dma((2,)),
            dma((chunks, 2)),
            dma((chunks, 2)),
        ],
        compiler_params=pltpu.CompilerParams(
            collective_id=0, has_side_effects=True, vmem_limit_bytes=60 * 1024 * 1024
        ),
        name="owned_columns",
    )(first_view_outputs, second_view_outputs)
    return pl.pallas_call(
        hand_out,
        out_shape=[
            jax.ShapeDtypeStruct(first_view_outputs.shape, bf16),
            jax.ShapeDtypeStruct(second_view_outputs.shape, bf16),
        ],
        in_specs=[any_spec] * 2,
        out_specs=[any_spec] * 2,
        scratch_shapes=[
            pltpu.VMEM(first_view_outputs.shape, bf16),
            pltpu.VMEM(second_view_outputs.shape, bf16),
            dma((2,)),
            dma((2,)),
        ],
        name="hand_out",
    )(*landed)


def shards(first_view_outputs, second_view_outputs):
    rows_a, width_a = first_view_outputs.shape
    rows_b, width_b = second_view_outputs.shape
    fits = (
        lax.axis_size("dp") == 8
        and lax.axis_size("feat") == 4
        and rows_a % 16 == 0
        and rows_b == 2 * rows_a
        and width_a == 2 * width_b
        and width_a % (GROUP * BLK) == 0
        and (8 * rows_a) % (4 * BLK) == 0
        and 8 * rows_a <= 1024
    )
    plan = owned_shards if fits else general_shards
    return plan(first_view_outputs, second_view_outputs)


def solution(mesh):
    placed = (P("dp", "feat"), P("feat", "dp"))
    return jax.shard_map(
        shards,
        mesh=mesh,
        in_specs=placed,
        out_specs=(P("dp", "feat"), P("feat", "dp")),
        check_vma=False,
    )
```

profile of v0, /device:TPU:1, one launch (start us, length us, event | category | flops | bytes accessed | tf_op | source)
XLA Modules:
  0.0 43.6 jit_solution(14195293231126395652)
XLA Ops:
  0.6 39.8 %owned_columns.1 = (bf16[64,2048]{1,0:T(8,128)(2,1)S(1)}, bf16[128,1024]{1,0:T(8,128)(2,1)S(1)}) custom-call(bf16[64,2048]{1,0:T(8,128)(2,1)} %a_ref.1, bf16[128,1024]{1,0:T(8,128)(2,1)} %b_ref.1), custom_call_target="tpu_custom_call" | custom-call | tf_op jit(solution)/shard_map/owned_columns/pallas_call | solution.py:505
  40.5 0.0 copy-start
  40.5 0.7 %copy-done = bf16[64,2048]{1,0:T(8,128)(2,1)} copy-done((bf16[64,2048]{1,0:T(8,128)(2,1)}, bf16[64,2048]{1,0:T(8,128)(2,1)S(1)}, u32[]{:S(2)}) %copy-start) | copy-done | bytes 262168
  41.2 0.0 copy-start.1
  41.2 0.7 %copy-done.1 = bf16[128,1024]{1,0:T(8,128)(2,1)} copy-done((bf16[128,1024]{1,0:T(8,128)(2,1)}, bf16[128,1024]{1,0:T(8,128)(2,1)S(1)}, u32[]{:S(2)}) %copy-start.1) | copy-done | bytes 262168
  41.9 1.8 %hand_out.1 = (bf16[64,2048]{1,0:T(8,128)(2,1)}, bf16[128,1024]{1,0:T(8,128)(2,1)}) custom-call(bf16[64,2048]{1,0:T(8,128)(2,1)} %copy-done, bf16[128,1024]{1,0:T(8,128)(2,1)} %copy-done.1), custom_call_target="tpu_custom_call" | custom-call | tf_op jit(solution)/shard_map/hand_out/pallas_call | solution.py:552
Async XLA Ops:
  40.5 0.7 %copy-start = (bf16[64,2048]{1,0:T(8,128)(2,1)}, bf16[64,2048]{1,0:T(8,128)(2,1)S(1)}, u32[]{:S(2)}) copy-start(bf16[64,2048]{1,0:T(8,128)(2,1)S(1)} %get-tuple-element.4.landed_a) | copy-start | bytes 786436
  41.2 0.7 %copy-start.1 = (bf16[128,1024]{1,0:T(8,128)(2,1)}, bf16[128,1024]{1,0:T(8,128)(2,1)S(1)}, u32[]{:S(2)}) copy-start(bf16[128,1024]{1,0:T(8,128)(2,1)S(1)} %get-tuple-element.5.landed_b) | copy-start | bytes 786436
where the time goes:
time: 43.8 us; the launch traced here: 43.6 us
  Pallas kernels  41.6 us (95%)
  local copies, waits for them, and re-layouts  1.39 us (3%)
  between operations  0.65 us (1%)
    pallas_call x1, Pallas kernels, owned_shards(): pl.pallas_call(functools.partial(kernel, float(features), chunk), out_sha...  39.8 us
    pallas_call x1, Pallas kernels, owned_shards(): pl.pallas_call(hand_out, out_shape=[jax.ShapeDtypeStruct(first_view_outpu...  1.77 us
    unnamed x4, local copies, waits for them, and re-layouts  1.39 us

commit v1 on v0

--- a/solution.py
+++ b/solution.py
@@ -472,21 +472,13 @@
     pltpu.make_async_copy(gb_ref, gb_ref, out_recv.at[1]).wait()
 
 
-def hand_out(landed_a, landed_b, ga_ref, gb_ref, held_a, held_b, loads, stores):
-    moves = ((landed_a, held_a, ga_ref), (landed_b, held_b, gb_ref))
-    fetched = [
-        pltpu.make_async_copy(src, held, loads.at[i]) for i, (src, held, _) in enumerate(moves)
-    ]
-    written = [
-        pltpu.make_async_copy(held, dst, stores.at[i]) for i, (_, held, dst) in enumerate(moves)
-    ]
-    for cp in fetched:
-        cp.start()
-    for first, second in zip(fetched, written):
-        first.wait()
-        second.start()
-    for cp in written:
-        cp.wait()
+def hand_out(landed_a, landed_b, ga_ref, gb_ref, stores):
+    first = pltpu.make_async_copy(landed_a, ga_ref, stores.at[0])
+    second = pltpu.make_async_copy(landed_b, gb_ref, stores.at[1])
+    first.start()
+    second.start()
+    first.wait()
+    second.wait()
 
 
 def owned_shards(first_view_outputs, second_view_outputs):
@@ -555,14 +547,10 @@
             jax.ShapeDtypeStruct(first_view_outputs.shape, bf16),
             jax.ShapeDtypeStruct(second_view_outputs.shape, bf16),
         ],
-        in_specs=[any_spec] * 2,
+        in_specs=[pl.BlockSpec(memory_space=pltpu.VMEM)] * 2,
         out_specs=[any_spec] * 2,
-        scratch_shapes=[
-            pltpu.VMEM(first_view_outputs.shape, bf16),
-            pltpu.VMEM(second_view_outputs.shape, bf16),
-            dma((2,)),
-            dma((2,)),
-        ],
+        scratch_shapes=[dma((2,))],
+        compiler_params=pltpu.CompilerParams(vmem_limit_bytes=4 * 1024 * 1024),
         name="hand_out",
     )(*landed)
 

time: 43.8 us -> 41.4 us (0.945)
  local copies, waits for them, and re-layouts: 1.39 us -> 0 us
  Pallas kernels: 41.6 us -> 40.6 us
    unnamed x4 -> x0, local copies, waits for them, and re-layouts: 1.39 us -> none
    pallas_call x1, Pallas kernels: 1.77 us -> 0.81 us  [owned_shards(): pl.pallas_call(hand_out, out_shape=[jax.ShapeDtypeStruct(first_view_outpu...]
where the time goes in v1:
time: 41.4 us; the launch traced here: 41.3 us
  Pallas kernels  40.6 us (98%)
  between operations  0.64 us (2%)
    pallas_call x1, Pallas kernels, owned_shards(): pl.pallas_call(functools.partial(kernel, float(features), chunk), out_sha...  39.8 us

profile of v1, /device:TPU:1, one launch (start us, length us, event | category | flops | bytes accessed | tf_op | source)
XLA Modules:
  0.0 41.3 jit_solution(15835021265780445449)
XLA Ops:
  0.6 39.8 %owned_columns.1 = (bf16[64,2048]{1,0:T(8,128)(2,1)S(1)}, bf16[128,1024]{1,0:T(8,128)(2,1)S(1)}) custom-call(bf16[64,2048]{1,0:T(8,128)(2,1)} %a_ref.1, bf16[128,1024]{1,0:T(8,128)(2,1)} %b_ref.1), custom_call_target="tpu_custom_call" | custom-call | tf_op jit(solution)/shard_map/owned_columns/pallas_call | solution.py:497
  40.5 0.8 %hand_out.1 = (bf16[64,2048]{1,0:T(8,128)(2,1)}, bf16[128,1024]{1,0:T(8,128)(2,1)}) custom-call(bf16[64,2048]{1,0:T(8,128)(2,1)S(1)} %get-tuple-element.4.landed_a, bf16[128,1024]{1,0:T(8,128)(2,1)S(1)} %get-tuple-element.5.landed_b), custom_call_target="tpu_custom_call" | custom-call | tf_op jit(solution)/shard_map/hand_out/pallas_call | solution.py:544

commit v2 on v1

--- a/solution.py
+++ b/solution.py
@@ -10,6 +10,7 @@
 OFF_WEIGHT = 0.0051
 MESH = pl.DeviceIdType.MESH
 BLK = 128
+HOMEWARD = (4, 3, 5, 2, 6, 1, 7, 8)
 GROUP = 4
 
 
@@ -133,8 +134,8 @@
     g = 2 * y + x
     rows_a = a_ref.shape[0]
     rows_b = b_ref.shape[0]
-    count, width = raw.shape
-    n_chunks = width // chunk
+    n_chunks, count, _ = raw.shape
+    width = n_chunks * chunk
     n_blk = count // BLK
     seg = packed.shape[0] // GROUP
     unit = seg // GROUP
@@ -182,9 +183,7 @@
         return a_ref.at[:, pl.ds(pl.multiple_of(q * width + c * chunk, chunk), chunk)]
 
     def rows_for_a(c):
-        return raw.at[
-            pl.ds(pl.multiple_of(p * rows_a, rows_a), rows_a), pl.ds(c * chunk, chunk)
-        ]
+        return raw.at[c, pl.ds(pl.multiple_of(p * rows_a, rows_a), rows_a), :]
 
     sent = []
     crossing = []
@@ -220,10 +219,7 @@
             sent.append(
                 start_or_local(
                     b_ref.at[:, pl.ds(pl.multiple_of(x_to * width + c * chunk, chunk), chunk)],
-                    raw.at[
-                        pl.ds(pl.multiple_of(f * rows_b, rows_b), rows_b),
-                        pl.ds(c * chunk, chunk),
-                    ],
+                    raw.at[c, pl.ds(pl.multiple_of(f * rows_b, rows_b), rows_b), :],
                     in_send.at[c, GROUP + k],
                     in_recv.at[c],
                     (p, feat_to),
@@ -257,24 +253,22 @@
             where[bi, bj] = len(where)
     swaps = []
     for c in range(n_chunks):
-        part = raw.at[:, pl.ds(c * chunk, chunk)]
-        pltpu.make_async_copy(part, part, in_recv.at[c]).wait()
-        for h in range(c * chunk, (c + 1) * chunk, BLK):
+        pltpu.make_async_copy(raw.at[c], raw.at[c], in_recv.at[c]).wait()
+        for h in range(0, chunk, BLK):
             cols = slice(h, h + BLK)
-            values = raw[:, cols].astype(jnp.float32)
+            values = raw[c, :, cols].astype(jnp.float32)
             center = jnp.sum(values, axis=0, keepdims=True) / count
             centered = values - center
             spread = jnp.sum(centered * centered, axis=0, keepdims=True) / count
             inverse = lax.rsqrt(spread + EPSILON)
             standardized = centered * inverse
-            xhat[:, cols] = standardized
-            norm[:, cols] = standardized.astype(jnp.bfloat16)
-            inv[0:1, cols] = inverse
-        cols = slice(c * chunk, (c + 1) * chunk)
+            xhat[c, :, cols] = standardized
+            norm[c, :, cols] = standardized.astype(jnp.bfloat16)
+            inv[c, 0:1, cols] = inverse
         for bi in range(n_blk):
             share = lax.dot_general(
-                norm[bi * BLK : (bi + 1) * BLK, cols],
-                norm[bi * BLK :, cols],
+                norm[c, bi * BLK : (bi + 1) * BLK, :],
+                norm[c, bi * BLK :, :],
                 (((1,), (1,)), ((), ())),
                 preferred_element_type=jnp.float32,
             )
@@ -290,8 +284,8 @@
                 else:
                     packed[at, :] = block.astype(jnp.bfloat16)
         swap = pltpu.make_async_remote_copy(
-            src_ref=norm.at[:, pl.ds(c * chunk, chunk)],
-            dst_ref=other.at[:, pl.ds(c * chunk, chunk)],
+            src_ref=norm.at[c],
+            dst_ref=other.at[c],
             send_sem=swap_send.at[c],
             recv_sem=swap_recv.at[c],
             device_id=(p, 2 * x + 1 - core),
@@ -384,12 +378,11 @@
     scale = 2.0 * OFF_WEIGHT / count
     for c in range(n_chunks):
         swaps[c].wait_recv()
-        cols = slice(c * chunk, (c + 1) * chunk)
-        own = norm[:, cols].astype(jnp.float32)
-        paired = other[:, cols].astype(jnp.float32)
+        own = norm[c].astype(jnp.float32)
+        paired = other[c].astype(jnp.float32)
         corr = jnp.sum(own * paired, axis=0, keepdims=True) / count
         diagonal = 2.0 * (corr - 1.0) - 2.0 * OFF_WEIGHT * corr
-        base[:, cols] = own * (scale * features) + paired * diagonal
+        base[c] = own * (scale * features) + paired * diagonal
     for cp in last:
         cp.wait_recv()
     for (bi, bj), at in where.items():
@@ -399,24 +392,23 @@
             gram[bj * BLK : (bj + 1) * BLK, bi * BLK : (bi + 1) * BLK] = block.T
 
     for c in range(n_chunks):
-        cols = slice(c * chunk, (c + 1) * chunk)
-        dnorm = base[:, cols] + scale * lax.dot_general(
-            gram[...], norm[:, cols], (((1,), (0,)), ((), ())), preferred_element_type=jnp.float32
-        )
-        standardized = xhat[:, cols]
+        dnorm = base[c] + scale * lax.dot_general(
+            gram[...], norm[c], (((1,), (0,)), ((), ())), preferred_element_type=jnp.float32
+        )
+        standardized = xhat[c]
         centering = jnp.sum(dnorm, axis=0, keepdims=True) / count
         projection = jnp.sum(dnorm * standardized, axis=0, keepdims=True) / count
-        grad[:, cols] = (
-            (dnorm - centering - standardized * projection) * inv[0:1, cols]
+        grad[c] = (
+            (dnorm - centering - standardized * projection) * inv[c, 0:1, :]
         ).astype(jnp.bfloat16)
 
         @pl.when(core == 0)
         def _():
             place = pl.ds(pl.multiple_of(g * width + c * chunk, chunk), chunk)
-            for k in range(1, n_dp + 1):
+            for k in HOMEWARD:
                 to = (p + k) % n_dp
                 is_self = jnp.logical_and(to == p, z == f)
-                src = grad.at[pl.ds(pl.multiple_of(to * rows_a, rows_a), rows_a), cols]
+                src = grad.at[c, pl.ds(pl.multiple_of(to * rows_a, rows_a), rows_a), :]
 
                 start_or_local(
                     src,
@@ -432,7 +424,7 @@
             place = pl.ds(pl.multiple_of(x * width + c * chunk, chunk), chunk)
             for k in range(1, n_feat + 1):
                 to = (f + k) % n_feat
-                src = grad.at[pl.ds(pl.multiple_of(to * rows_b, rows_b), rows_b), cols]
+                src = grad.at[c, pl.ds(pl.multiple_of(to * rows_b, rows_b), rows_b), :]
                 if k == n_feat:
                     pltpu.make_async_copy(src, gb_ref.at[:, place], out_recv.at[1]).start()
                 else:
@@ -455,7 +447,7 @@
         for c in range(n_chunks):
             for k in range(1, n_dp + 1):
                 to = (p + k) % n_dp
-                piece = grad.at[0:rows_a, 0:chunk]
+                piece = grad.at[c, 0:rows_a, :]
 
                 @pl.when(jnp.logical_not(jnp.logical_and(to == p, z == f)))
                 def _():
@@ -465,7 +457,7 @@
     def _():
         for c in range(n_chunks):
             for k in range(1, n_feat):
-                piece = grad.at[0:rows_b, 0:chunk]
+                piece = grad.at[c, 0:rows_b, :]
                 pltpu.make_async_copy(piece, piece, out_send.at[c, k - 1]).wait()
 
     pltpu.make_async_copy(ga_ref, ga_ref, out_recv.at[0]).wait()
@@ -503,12 +495,12 @@
         in_specs=[any_spec] * 2,
         out_specs=[pl.BlockSpec(memory_space=pltpu.VMEM)] * 2,
         scratch_shapes=[
-            pltpu.VMEM((count, width), bf16),
-            pltpu.VMEM((count, width), f32),
-            pltpu.VMEM((8, width), f32),
-            pltpu.VMEM((count, width), bf16),
-            pltpu.VMEM((count, width), bf16),
-            pltpu.VMEM((count, width), f32),
+            pltpu.VMEM((chunks, count, chunk), bf16),
+            pltpu.VMEM((chunks, count, chunk), f32),
+            pltpu.VMEM((chunks, 8, chunk), f32),
+            pltpu.VMEM((chunks, count, chunk), bf16),
+            pltpu.VMEM((chunks, count, chunk), bf16),
+            pltpu.VMEM((chunks, count, chunk), f32),
             pltpu.VMEM((packed_rows, BLK), f32),
             pltpu.VMEM((packed_rows, BLK), bf16),
             pltpu.VMEM((GROUP, GROUP - 1, unit, BLK), bf16),
@@ -517,7 +509,7 @@
             pltpu.VMEM((seg, BLK), bf16),
             pltpu.VMEM((packed_rows, BLK), bf16),
             pltpu.VMEM((count, count), bf16),
-            pltpu.VMEM((count, width), bf16),
+            pltpu.VMEM((chunks, count, chunk), bf16),
             pltpu.VMEM((chunks, 2, first_view_outputs.shape[0], chunk), bf16),
             dma((chunks, GROUP + 2)),
             dma((chunks,)),

time: 41.4 us -> 40.9 us (0.988)
  Pallas kernels: 40.6 us -> 40.1 us
    pallas_call x1, Pallas kernels: 39.8 us -> 39.3 us  [owned_shards(): pl.pallas_call(functools.partial(kernel, float(features), chunk), out_sha...]
where the time goes in v2:
time: 40.9 us; the launch traced here: 40.7 us
  Pallas kernels  40.1 us (98%)
  between operations  0.64 us (2%)
    pallas_call x1, Pallas kernels, owned_shards(): pl.pallas_call(functools.partial(kernel, float(features), chunk), out_sha...  39.3 us

profile of v2, /device:TPU:1, one launch (start us, length us, event | category | flops | bytes accessed | tf_op | source)
XLA Modules:
  0.0 40.7 jit_solution(8116561080645551375)
XLA Ops:
  0.6 39.3 %owned_columns.1 = (bf16[64,2048]{1,0:T(8,128)(2,1)S(1)}, bf16[128,1024]{1,0:T(8,128)(2,1)S(1)}) custom-call(bf16[64,2048]{1,0:T(8,128)(2,1)} %a_ref.1, bf16[128,1024]{1,0:T(8,128)(2,1)} %b_ref.1), custom_call_target="tpu_custom_call" | custom-call | tf_op jit(solution)/shard_map/owned_columns/pallas_call | solution.py:489
  39.9 0.8 %hand_out.1 = (bf16[64,2048]{1,0:T(8,128)(2,1)}, bf16[128,1024]{1,0:T(8,128)(2,1)}) custom-call(bf16[64,2048]{1,0:T(8,128)(2,1)S(1)} %get-tuple-element.4.landed_a, bf16[128,1024]{1,0:T(8,128)(2,1)S(1)} %get-tuple-element.5.landed_b), custom_call_target="tpu_custom_call" | custom-call | tf_op jit(solution)/shard_map/hand_out/pallas_call | solution.py:536

commit v3 on v2

--- a/solution.py
+++ b/solution.py
@@ -187,13 +187,15 @@
 
     sent = []
     crossing = []
+    straight = []
+    relayed = [2] * (n_chunks - 1) + [1]
     for c in range(n_chunks):
-        for ys in range(2):
+        for k in range(relayed[c]):
             cp = pltpu.make_async_remote_copy(
-                src_ref=piece_of_a(c, 2 * ys + 1 - x),
-                dst_ref=relay.at[c, ys],
-                send_sem=relay_send.at[c, ys],
-                recv_sem=relay_recv.at[c, ys],
+                src_ref=piece_of_a(c, 2 * ((y + 1 + k) % 2) + 1 - x),
+                dst_ref=relay.at[c, k],
+                send_sem=relay_send.at[c, k],
+                recv_sem=relay_recv.at[c, k],
                 device_id=(p, 2 * (1 - x) + core),
                 device_id_type=MESH,
             )
@@ -212,6 +214,18 @@
                     jnp.logical_and(dp_to == p, core == 0),
                 )
             )
+        for k in range(relayed[c], 2):
+            y_to = (y + 1 + k) % 2
+            cp = pltpu.make_async_remote_copy(
+                src_ref=piece_of_a(c, 2 * y_to + 1 - x),
+                dst_ref=rows_for_a(c),
+                send_sem=in_send.at[c, 2 + k],
+                recv_sem=in_recv.at[c],
+                device_id=(2 * f + y_to, 2 * (1 - x)),
+                device_id_type=MESH,
+            )
+            cp.start()
+            straight.append(cp)
     for c in range(n_chunks):
         for k in range(2):
             x_to = (x + 1 + k) % 2
@@ -227,14 +241,14 @@
                 )
             )
     for c in range(n_chunks):
-        for ys in range(2):
-            crossing[2 * c + ys].wait_recv()
-            dp_to = 2 * (2 * (1 - x) + core) + ys
+        for k in range(relayed[c]):
+            crossing[sum(relayed[:c]) + k].wait_recv()
+            dp_to = 2 * (2 * (1 - x) + core) + (y + 1 + k) % 2
             sent.append(
                 start_or_local(
-                    relay.at[c, ys],
+                    relay.at[c, k],
                     rows_for_a(c),
-                    in_send.at[c, 2 + ys],
+                    in_send.at[c, 2 + k],
                     in_recv.at[c],
                     (dp_to, 2 * x),
                     jnp.logical_and(dp_to == p, core == 0),
@@ -439,7 +453,7 @@
 
     for item in sent:
         wait_sent(item)
-    for cp in crossing + swaps + copies + last:
+    for cp in crossing + straight + swaps + copies + last:
         cp.wait_send()
 
     @pl.when(core == 0)

time: 40.9 us -> 40.1 us (0.980)
  Pallas kernels: 40.1 us -> 39.3 us
    pallas_call x1, Pallas kernels: 39.3 us -> 38.5 us  [owned_shards(): pl.pallas_call(functools.partial(kernel, float(features), chunk), out_sha...]
where the time goes in v3:
time: 40.1 us; the launch traced here: 39.9 us
  Pallas kernels  39.3 us (98%)
  between operations  0.64 us (2%)
    pallas_call x1, Pallas kernels, owned_shards(): pl.pallas_call(functools.partial(kernel, float(features), chunk), out_sha...  38.5 us
    pallas_call x1, Pallas kernels, owned_shards(): pl.pallas_call(hand_out, out_shape=[jax.ShapeDtypeStruct(first_view_outpu...  0.81 us

profile of v3, /device:TPU:1, one launch (start us, length us, event | category | flops | bytes accessed | tf_op | source)
XLA Modules:
  0.0 39.9 jit_solution(8287164578776418)
XLA Ops:
  0.6 38.5 %owned_columns.1 = (bf16[64,2048]{1,0:T(8,128)(2,1)S(1)}, bf16[128,1024]{1,0:T(8,128)(2,1)S(1)}) custom-call(bf16[64,2048]{1,0:T(8,128)(2,1)} %a_ref.1, bf16[128,1024]{1,0:T(8,128)(2,1)} %b_ref.1), custom_call_target="tpu_custom_call" | custom-call | tf_op jit(solution)/shard_map/owned_columns/pallas_call | solution.py:503
  39.1 0.8 %hand_out.1 = (bf16[64,2048]{1,0:T(8,128)(2,1)}, bf16[128,1024]{1,0:T(8,128)(2,1)}) custom-call(bf16[64,2048]{1,0:T(8,128)(2,1)S(1)} %get-tuple-element.4.landed_a, bf16[128,1024]{1,0:T(8,128)(2,1)S(1)} %get-tuple-element.5.landed_b), custom_call_target="tpu_custom_call" | custom-call | tf_op jit(solution)/shard_map/hand_out/pallas_call | solution.py:550

commit v4 on v3

--- a/solution.py
+++ b/solution.py
@@ -188,7 +188,7 @@
     sent = []
     crossing = []
     straight = []
-    relayed = [2] * (n_chunks - 1) + [1]
+    relayed = [2] * (n_chunks - n_chunks // 2) + [1] * (n_chunks // 2)
     for c in range(n_chunks):
         for k in range(relayed[c]):
             cp = pltpu.make_async_remote_copy(
@@ -491,7 +491,7 @@
     count = first_view_outputs.shape[0] * lax.axis_size("dp")
     features = first_view_outputs.shape[1] * lax.axis_size("feat")
     width = first_view_outputs.shape[1] // GROUP
-    chunk = 256 if width % 256 == 0 else 128
+    chunk = BLK
     chunks = width // chunk
     n_blk = count // BLK
     packed_rows = n_blk * (n_blk + 1) // 2 * BLK

time: 40.1 us -> 40.7 us (1.015)
  no operation moved by 1% of the time
where the time goes in v4:
time: 40.7 us; the launch traced here: 40.3 us
  Pallas kernels  39.7 us (98%)
  between operations  0.64 us (2%)
    pallas_call x1, Pallas kernels, owned_shards(): pl.pallas_call(functools.partial(kernel, float(features), chunk), out_sha...  38.9 us

profile of v4, /device:TPU:1, one launch (start us, length us, event | category | flops | bytes accessed | tf_op | source)
XLA Modules:
  0.0 40.3 jit_solution(15363437747026255665)
XLA Ops:
  0.6 38.9 %owned_columns.1 = (bf16[64,2048]{1,0:T(8,128)(2,1)S(1)}, bf16[128,1024]{1,0:T(8,128)(2,1)S(1)}) custom-call(bf16[64,2048]{1,0:T(8,128)(2,1)} %a_ref.1, bf16[128,1024]{1,0:T(8,128)(2,1)} %b_ref.1), custom_call_target="tpu_custom_call" | custom-call | tf_op jit(solution)/shard_map/owned_columns/pallas_call | solution.py:503
  39.5 0.8 %hand_out.1 = (bf16[64,2048]{1,0:T(8,128)(2,1)}, bf16[128,1024]{1,0:T(8,128)(2,1)}) custom-call(bf16[64,2048]{1,0:T(8,128)(2,1)S(1)} %get-tuple-element.4.landed_a, bf16[128,1024]{1,0:T(8,128)(2,1)S(1)} %get-tuple-element.5.landed_b), custom_call_target="tpu_custom_call" | custom-call | tf_op jit(solution)/shard_map/hand_out/pallas_call | solution.py:550
